TPU v7x, 256 devices: a whole 4x4x8 slice. The times are simulated.
256 devices in a mesh: ctx: 32 (over y_lo, z, core), head: 8 (over y_hi, x).
Axes of the slice: x: 4, y: 4 (y_hi: 2, y_lo: 2; y = y_hi * 2 + y_lo), z: 8, core: 2. Of those that a mesh axis runs over, the one named last changes fastest.
Arguments:
- q_nope: bfloat16 [8192, 128, 128], P('ctx', 'head'), may hold values from -6 to 6
- q_rope: bfloat16 [8192, 8192], P('ctx', 'head'), may hold values from -400 to 400
- latent: bfloat16 [8192, 576], P('ctx'), may hold values from -8 to 8
- w_uk: bfloat16 [512, 128, 128], P(None, 'head'), may hold values from -0.25 to 0.25
- w_uv: bfloat16 [512, 128, 128], P(None, 'head'), may hold values from -0.25 to 0.25
- span_order: int32 [64], replicated, may hold values from 0 to 63, each once
Outputs:
- attended: bfloat16 [8192, 128, 128], P('ctx', 'head')
- log_total: float32 [128, 8192], P('head', 'ctx')
All inputs are finite; a program needn't handle non-finite values.
Results may differ from a plain program's by a relative error of at most 0.0059.
Values may be sent and summed in bfloat16 or wider, within the bound.
No kernel may reach another device: no remote copies, remote signals or barrier semaphores. Data moves between devices by JAX's collectives and lax.ppermute only.
A program may use at most 128 MiB of HBM per device.

v0:
```python
import jax
import jax.numpy as jnp
from jax import lax
from jax.sharding import PartitionSpec as P

HOPS = 2


def from_behind(block, axis, distance):
    devices = range(lax.axis_size(axis))
    route = [((i - distance) % len(devices), i) for i in devices]
    return lax.ppermute(block, axis, route)


def positions(span_order, device, rows):
    half = rows // 2
    offsets = jnp.arange(rows, dtype=jnp.int32)
    pair = lax.dynamic_slice_in_dim(span_order, 2 * device, 2, 0)
    span = jnp.where(offsets < half, pair[0], pair[1])
    return span * half + offsets % half


def local(q_nope, q_rope, latent, w_uk, w_uv, span_order):
    rows = latent.shape[0]
    width = w_uk.shape[0]
    heads_here = w_uk.shape[1]
    rope_width = latent.shape[1] - width
    cycle = lax.axis_size("ctx")
    device = lax.axis_index("ctx")
    forward_steps = list(range(1, HOPS + 1))
    backward_steps = [-k for k in range(1, HOPS + 1)]
    forward_list, backward_list = ([], [])
    forward = latent
    backward = latent
    for hop in range(HOPS):
        forward = from_behind(forward, "ctx", 1)
        backward = from_behind(backward, "ctx", -1)
        forward_list.append(forward)
        backward_list.append(backward)
    arrived = forward_list + backward_list
    keys = jnp.concatenate([latent] + arrived, 0)
    query_pos = positions(span_order, device, rows)
    pos_list = [query_pos]
    for step in forward_steps + backward_steps:
        pos_list.append(positions(span_order, (device - step) % cycle, rows))
    key_pos = jnp.concatenate(pos_list, 0)
    compressed = keys[:, :width]
    keys_nope = jnp.einsum(
        "tc,chd->thd", compressed, w_uk, preferred_element_type=jnp.float32
    ).astype(jnp.bfloat16)
    values = jnp.einsum("tc,chd->thd", compressed, w_uv, preferred_element_type=jnp.float32).astype(
        jnp.bfloat16
    )
    query_rot = q_rope.reshape(rows, heads_here, rope_width)
    scores = jnp.einsum("qhd,khd->hqk", q_nope, keys_nope, preferred_element_type=jnp.float32)
    scores = scores + jnp.einsum(
        "qhr,kr->hqk", query_rot, keys[:, width:], preferred_element_type=jnp.float32
    )
    scores = scores * (1.0 / (q_nope.shape[2] + rope_width) ** 0.5)
    visible = (key_pos[None, :] <= query_pos[:, None])[None]
    scores = jnp.where(visible, scores, -jnp.inf)
    top = jnp.max(scores, axis=2, keepdims=True)
    expo = jnp.exp(scores - top)
    total = jnp.sum(expo, axis=2, keepdims=True)
    weights = (expo / total).astype(jnp.bfloat16)
    attended = jnp.einsum(
        "hqk,khd->qhd", weights, values, preferred_element_type=jnp.float32
    ).astype(jnp.bfloat16)
    log_total = (top + jnp.log(total))[:, :, 0]
    return (attended, log_total)


def solution(mesh):
    return jax.shard_map(
        local,
        mesh=mesh,
        in_specs=(
            P("ctx", "head", None),
            P("ctx", "head"),
            P("ctx", None),
            P(None, "head", None),
            P(None, "head", None),
            P(),
        ),
        out_specs=(P("ctx", "head", None), P("head", "ctx")),
        check_vma=False,
    )
```

profile of v0, /device:TPU:2, one launch (start us, length us, event | category | flops | bytes accessed | tf_op | source)
XLA Modules:
  0.0 76.7 jit_solution(9815421626563385602)
XLA Ops:
  0.6 0.0 copy-start
  0.6 0.1 collective-permute-start
  0.7 6.4 %collective-permute-start.2 = (bf16[256,576]{0,1:T(8,128)(2,1)}, bf16[256,576]{0,1:T(8,128)(2,1)S(1)}, u32[]{:S(2)}, u32[]{:S(2)}) collective-permute-start(bf16[256,576]{0,1:T(8,128)(2,1)} %param.8), channel_id=1, source_target_pairs={{8,0},{16,8},{24,16},{32,24},{40,32},{48,40},{56,48},{64,56},{72,6... | collective-permute-start | bytes 884744 | tf_op jit(solution)/shard_map/ppermute | solution.py:12
  7.1 0.9 %fusion.17 = (s32[2]{0:T(128)S(1)}, s32[2]{0:T(128)S(1)}, s32[2]{0:T(128)S(1)}, s32[2]{0:T(128)S(1)}, s32[2]{0:T(128)S(1)}) fusion(s32[64]{0:T(128)} %param.11, s32[]{:T(128)S(6)} %select_n.97, s32[]{:T(128)S(6)} %select_n.91, s32[]{:T(128)S(6)} %select_n.88, s32[]{:T(128)S(6)} %select_n.84, s32[]{:T(128)S(6)} %select_n.94), kind=kLoop, calls=%fused_computation.33 | loop fusion | bytes 100 | tf_op jit(solution)/shard_map/dynamic_slice | solution.py:18
  8.0 0.6 fusion.21
  8.6 1.3 %multiply_add_fusion = s32[256]{0:T(256)S(1)} fusion(s32[]{:T(128)} %bitcast.2, s32[]{:T(128)} %bitcast.1), kind=kLoop, calls=%fused_computation.30 | loop fusion | flops 2560 | bytes 1032 | tf_op jit(solution)/shard_map/add | solution.py:20
  9.9 1.3 %constant_dynamic-update-slice_fusion.5 = s32[1280]{0:T(1024)S(1)} fusion(s32[1280]{0:T(1024)S(1)} %custom-call, s32[]{:T(128)} %bitcast.2, s32[]{:T(128)} %bitcast.1), kind=kLoop, calls=%fused_computation.24 | loop fusion | flops 2560 | bytes 1032
  11.2 0.7 fusion.16
  11.9 0.7 fusion.19
  12.6 1.3 %constant_dynamic-update-slice_fusion.9 = s32[1280]{0:T(1024)S(1)} fusion(s32[1280]{0:T(1024)S(1)} %constant_dynamic-update-slice_fusion.5, s32[]{:T(128)} %bitcast.4, s32[]{:T(128)} %bitcast.3), kind=kLoop, calls=%fused_computation.28 | loop fusion | flops 2560 | bytes 1032
  13.9 1.3 %constant_dynamic-update-slice_fusion.8 = s32[1280]{0:T(1024)S(1)} fusion(s32[1280]{0:T(1024)S(1)} %constant_dynamic-update-slice_fusion.9, s32[]{:T(128)} %bitcast.6, s32[]{:T(128)} %bitcast.5), kind=kLoop, calls=%fused_computation.27 | loop fusion | flops 2560 | bytes 1032
  15.2 1.3 %constant_dynamic-update-slice_fusion.7 = s32[1280]{0:T(1024)S(1)} fusion(s32[1280]{0:T(1024)S(1)} %constant_dynamic-update-slice_fusion.8, s32[]{:T(128)} %bitcast.8, s32[]{:T(128)} %bitcast.7), kind=kLoop, calls=%fused_computation.26 | loop fusion | flops 2560 | bytes 1032
  16.4 1.2 %constant_dynamic-update-slice_fusion.6 = s32[1280]{0:T(1024)S(1)} fusion(s32[1280]{0:T(1024)S(1)} %constant_dynamic-update-slice_fusion.7, s32[]{:T(128)} %bitcast.10, s32[]{:T(128)} %bitcast.9), kind=kLoop, calls=%fused_computation.25 | loop fusion | flops 2560 | bytes 1032 | tf_op jit(solution)/shard_map/concatenate | solution.py:46
  17.6 0.0 collective-permute-done
  17.6 0.1 collective-permute-start.1
  17.7 0.2 broadcast_compare_fusion
  18.0 1.2 %copy.13 = bf16[256,1024]{0,1:T(8,128)(2,1)S(1)} copy(bf16[256,1024]{1,0:T(8,128)(2,1)} %param.7) | data formatting | bytes 1048576 | tf_op args[1]
  19.2 1.7 %constant_dynamic-update-slice_fusion.4 = bf16[1280,576]{0,1:T(8,128)(2,1)} fusion(bf16[256,576]{0,1:T(8,128)(2,1)} %param.8), kind=kLoop, calls=%fused_computation.23 | loop fusion | bytes 589824
  21.0 0.0 collective-permute-done.2
  21.0 3.8 %collective-permute-start.3 = (bf16[256,576]{0,1:T(8,128)(2,1)S(1)}, bf16[256,576]{0,1:T(8,128)(2,1)S(1)}, u32[]{:S(2)}, u32[]{:S(2)}) collective-permute-start(bf16[256,576]{0,1:T(8,128)(2,1)S(1)} %collective-permute-done.2), channel_id=1, source_target_pairs={{8,0},{16,8},{24,16},{32,24},{40,32},{48,40},{56,48},{64,56},{72,6... | collective-permute-start | bytes 884744 | tf_op jit(solution)/shard_map/ppermute | solution.py:12
  24.8 0.8 %constant_dynamic-update-slice_fusion.3 = bf16[1280,576]{0,1:T(8,128)(2,1)} fusion(bf16[1280,576]{0,1:T(8,128)(2,1)} %constant_dynamic-update-slice_fusion.4, bf16[256,576]{0,1:T(8,128)(2,1)S(1)} %collective-permute-done), kind=kLoop, calls=%fused_computation.22 | loop fusion | bytes 589824
  25.6 0.5 collective-permute-done.1
  26.1 1.8 %constant_dynamic-update-slice_fusion.2 = bf16[1280,576]{0,1:T(8,128)(2,1)} fusion(bf16[1280,576]{0,1:T(8,128)(2,1)} %constant_dynamic-update-slice_fusion.3, bf16[256,576]{0,1:T(8,128)(2,1)} %collective-permute-done.1), kind=kLoop, calls=%fused_computation.21 | loop fusion | bytes 589824
  27.8 0.8 %constant_dynamic-update-slice_fusion.1 = bf16[1280,576]{0,1:T(8,128)(2,1)} fusion(bf16[1280,576]{0,1:T(8,128)(2,1)} %constant_dynamic-update-slice_fusion.2, bf16[256,576]{0,1:T(8,128)(2,1)S(1)} %collective-permute-done.2), kind=kLoop, calls=%fused_computation.20 | loop fusion | bytes 589824
  28.6 0.4 collective-permute-done.3
  29.0 0.8 constant_dynamic-update-slice_fusion
  29.8 0.0 copy-done
  29.8 11.4 %fusion.4 = f32[16,1280,256]{2,1,0:T(8,128)} fusion(bf16[512,16,128]{2,1,0:T(8,128)(2,1)S(1)} %copy-done, bf16[256,16,128]{2,1,0:T(8,128)(2,1)} %param.6, bf16[1280,576]{0,1:T(8,128)(2,1)} %constant_dynamic-update-slice_fusion), kind=kOutput, calls=%fused_computation.9 | convolution fusion | flops 4029153280 | bytes 25427968 | tf_op jit(solution)/shard_map/qhd,khd->hqk/dot_general | solution.py:55
  41.2 13.2 %fusion.22 = (f32[16,256]{1,0:T(8,128)S(1)}, f32[16,256,1280]{1,2,0:T(8,128)}) fusion(bf16[256,16,64]{0,2,1:T(8,128)(2,1)S(1)} %bitcast.33, bf16[1280,576]{0,1:T(8,128)(2,1)} %constant_dynamic-update-slice_fusion, f32[16,1280,256]{2,1,0:T(8,128)} %fusion.4, pred[256,1280]{0,1:T(8,128)(4,1)S(1)} %broadcast_compare_fusion), kind=kOutput, calls=%fused_computation.38 | convolution fusion | flops 692056064 | bytes 42975232 | tf_op jit(solution)/shard_map/qhr,kr->hqk/dot_general | solution.py:56
  54.4 8.7 %fusion.2 = f32[16,256]{1,0:T(8,128)S(1)} fusion(f32[16,256,1280]{1,2,0:T(8,128)} %get-tuple-element.22, f32[16,256]{1,0:T(8,128)S(1)} %get-tuple-element.21), kind=kLoop, calls=%fused_computation.5 | loop fusion | flops 10481664 | bytes 21004288 | tf_op jit(solution)/shard_map/reduce_sum | solution.py:64
  63.1 0.6 log_add_fusion
  63.7 11.2 %fusion.12 = bf16[256,16,128]{0,2,1:T(8,128)(2,1)S(1)} fusion(f32[16,256,1280]{1,2,0:T(8,128)} %get-tuple-element.22, f32[16,256]{1,0:T(8,128)S(1)} %fusion.2, f32[16,256]{1,0:T(8,128)S(1)} %get-tuple-element.21, bf16[512,16,128]{2,1,0:T(8,128)(2,1)} %param.10, bf16[1280,576]{0,1:T(8,128)(2,1)} %constant_dynamic-update-slice_fusion), kind=kOutput, calls=%fused_computation.13 | convolution fusion | flops 4045406208 | bytes 25460736 | tf_op jit(solution)/shard_map/hqk,khd->qhd/dot_general | solution.py:66
  74.9 1.8 %copy.15 = bf16[256,16,128]{2,1,0:T(8,128)(2,1)} copy(bf16[256,16,128]{0,2,1:T(8,128)(2,1)S(1)} %fusion.12) | data formatting | bytes 2097152
  (1 shorter events, 0.0 us)
Async XLA Ops:
  0.6 29.2 %copy-start = (bf16[512,16,128]{2,1,0:T(8,128)(2,1)S(1)}, bf16[512,16,128]{2,1,0:T(8,128)(2,1)}, u32[]{:S(2)}) copy-start(bf16[512,16,128]{2,1,0:T(8,128)(2,1)} %param.9) | copy-start | bytes 6291460
  0.6 17.0 %collective-permute-start = (bf16[256,576]{0,1:T(8,128)(2,1)}, bf16[256,576]{0,1:T(8,128)(2,1)S(1)}, u32[]{:S(2)}, u32[]{:S(2)}) collective-permute-start(bf16[256,576]{0,1:T(8,128)(2,1)} %param.8), channel_id=1, source_target_pairs={{248,0},{0,8},{8,16},{16,24},{24,32},{32,40},{40,48},{48,56},{56,6... | collective-permute-start | bytes 884744 | tf_op jit(solution)/shard_map/ppermute | solution.py:12
  0.7 20.2 %collective-permute-start.2 = (bf16[256,576]{0,1:T(8,128)(2,1)}, bf16[256,576]{0,1:T(8,128)(2,1)S(1)}, u32[]{:S(2)}, u32[]{:S(2)}) collective-permute-start(bf16[256,576]{0,1:T(8,128)(2,1)} %param.8), channel_id=1, source_target_pairs={{8,0},{16,8},{24,16},{32,24},{40,32},{48,40},{56,48},{64,56},{72,6... | collective-permute-start | bytes 884744 | tf_op jit(solution)/shard_map/ppermute | solution.py:12
  17.6 8.4 %collective-permute-start.1 = (bf16[256,576]{0,1:T(8,128)(2,1)S(1)}, bf16[256,576]{0,1:T(8,128)(2,1)}, u32[]{:S(2)}, u32[]{:S(2)}) collective-permute-start(bf16[256,576]{0,1:T(8,128)(2,1)S(1)} %collective-permute-done), channel_id=1, source_target_pairs={{248,0},{0,8},{8,16},{16,24},{24,32},{32,40},{40,48},{48,56},{56,6... | collective-permute-start | bytes 884744 | tf_op jit(solution)/shard_map/ppermute | solution.py:12
  21.0 8.1 %collective-permute-start.3 = (bf16[256,576]{0,1:T(8,128)(2,1)S(1)}, bf16[256,576]{0,1:T(8,128)(2,1)S(1)}, u32[]{:S(2)}, u32[]{:S(2)}) collective-permute-start(bf16[256,576]{0,1:T(8,128)(2,1)S(1)} %collective-permute-done.2), channel_id=1, source_target_pairs={{8,0},{16,8},{24,16},{32,24},{40,32},{48,40},{56,48},{64,56},{72,6... | collective-permute-start | bytes 884744 | tf_op jit(solution)/shard_map/ppermute | solution.py:12
where the time goes:
time: 77.1 us; the launch traced here: 76.7 us
  matrix products  35.8 us (46%)
  other arithmetic  17.2 us (22%)
  local copies, waits for them, and re-layouts  11.7 us (15%)
  starting transfers between devices  10.4 us (13%)
  waiting for transfers between devices  0.93 us (1%)
    dot_general x1, matrix products, local(): jnp.einsum('qhr,kr->hqk', query_rot, keys[:, width:], preferred_element_t...  13.2 us
    dot_general x1, matrix products, local(): jnp.einsum('qhd,khd->hqk', q_nope, keys_nope, preferred_element_type=jnp....  11.4 us
    dot_general x1, matrix products, local(): jnp.einsum('hqk,khd->qhd', weights, values, preferred_element_type=jnp.fl...  11.2 us
    ppermute x4, starting transfers between devices, from_behind(): return lax.ppermute(block, axis, route)  10.4 us
    reduce_sum x1, other arithmetic, local(): total = jnp.sum(expo, axis=2, keepdims=True)  8.68 us
    unnamed x8, local copies, waits for them, and re-layouts  8.09 us
    unnamed x5, other arithmetic  5.17 us
    slice x3, local copies, waits for them, and re-layouts, positions(): span = jnp.where(offsets < half, pair[0], pair[1])  1.91 us
  transfers between devices with their start and end apart: 4, of which 2 were waited for; matrix products, arithmetic and copies ran while one was open for 22% of the time, Pallas kernels for 0%

commit v1 on v0

v1 whole, which is shorter than its diff:
```python
import functools
import math

import jax
import jax.numpy as jnp
from jax import lax
from jax.experimental import pallas as pl
from jax.experimental.pallas import tpu as pltpu
from jax.sharding import PartitionSpec as P

ROWS = 256
HALF = 128
HEADS = 16
NOPE = 128
ROPE = 64
LATENT = 512
PAIRS = HEADS // 2
HIDDEN = -1e30
BF = jnp.bfloat16
F32 = jnp.float32
SCALE = 1.0 / (NOPE + ROPE) ** 0.5
TO_BASE2 = SCALE * math.log2(math.e)
SLOTS = 4


def dot(a, b):
    return jnp.dot(a, b, preferred_element_type=F32)


def dot_nt(a, b):
    return lax.dot_general(a, b, (((1,), (1,)), ((), ())), preferred_element_type=F32)


def partner(kind, i, cycle):
    chip = i // 2
    if kind == "mate":
        step = 1 - 2 * (i % 2)
    elif kind == "cross":
        step = 2 * (i % 2) - 1
    elif kind == "even":
        step = 2 - 4 * (chip % 2)
    elif kind == "odd":
        step = 4 * (chip % 2) - 2
    else:
        step = 0
    return (i + step + cycle) % cycle


def exchange(block, kind):
    cycle = lax.axis_size("ctx")
    return lax.ppermute(block, "ctx", [(partner(kind, i, cycle), i) for i in range(cycle)])


def prepare_block(span_ref, me, cycle, kind, turned, lat, ext, start):
    there = partner(kind, me, cycle)
    lane = lax.broadcasted_iota(jnp.int32, (ROPE, ROWS), 1)
    row = lax.broadcasted_iota(jnp.int32, (ROPE, ROWS), 0)
    span = jnp.where(lane < HALF, span_ref[2 * there], span_ref[2 * there + 1])
    mine = jnp.where(row == 0, span_ref[2 * me], span_ref[2 * me + 1])
    bias = jnp.where((row < 2) & (span > mine), HIDDEN, 0.0).astype(BF)
    lat[start : start + ROWS] = turned[:LATENT].T
    ext[start : start + ROWS] = jnp.concatenate([turned[LATENT:], bias], 0).T


def attend(keys, own, weights_k, weights_v, queries, lat, ext, scratch, before, finish):
    k_buf, v_buf, s_buf, p_buf, m_buf = scratch
    ones = jnp.ones((keys, NOPE), BF)
    if own:
        q_at = lax.broadcasted_iota(jnp.int32, (ROWS, ROWS), 0)
        k_at = lax.broadcasted_iota(jnp.int32, (ROWS, ROWS), 1)
        later = (q_at // HALF == k_at // HALF) & (k_at > q_at)
        own_bias = jnp.where(later, HIDDEN, 0.0).astype(F32)

    def project(pair):
        k_buf[pair % SLOTS] = dot(lat[...], weights_k(pair)).astype(BF)
        v_buf[pair % SLOTS] = dot(lat[...], weights_v(pair)).astype(BF)

    def score(pair):
        for j in range(2):
            head = 2 * pair + j
            part = k_buf[pair % SLOTS, :, j * NOPE : (j + 1) * NOPE]
            scores = dot_nt(queries[head], jnp.concatenate([part, ext[...]], 1))
            if own:
                scores = scores + own_bias
            s_buf[pair % 2, j] = scores
            top = jnp.max(scores, axis=1, keepdims=True)
            if before is not None:
                top = jnp.maximum(top, before(head)[0])
            m_buf[pair % SLOTS, j] = jnp.broadcast_to(top, (ROWS, NOPE))

    def weigh(pair):
        for j in range(2):
            top = m_buf[pair % SLOTS, j][:, :1]
            p_buf[pair % 2, j] = jnp.exp2((s_buf[pair % 2, j] - top) * TO_BASE2).astype(BF)

    def combine(pair):
        for j in range(2):
            head = 2 * pair + j
            part = v_buf[pair % SLOTS, :, j * NOPE : (j + 1) * NOPE]
            both = dot(p_buf[pair % 2, j], jnp.concatenate([part, ones], 1))
            total, acc = both[:, NOPE:], both[:, :NOPE]
            top = m_buf[pair % SLOTS, j]
            if before is not None:
                top0, total0, acc0 = before(head)
                fade = jnp.exp2((top0 - top) * TO_BASE2)
                total = total + total0 * fade
                acc = acc + acc0 * fade
            finish(head, top, total, acc)

    for step in range(-2, PAIRS + 1):
        for stage, ahead in ((combine, -1), (weigh, 0), (score, 1), (project, 2)):
            if 0 <= step + ahead < PAIRS:
                stage(step + ahead)


def scratch_for(keys):
    return [
        pltpu.VMEM((keys, LATENT), BF),
        pltpu.VMEM((keys, NOPE), BF),
        pltpu.VMEM((SLOTS, keys, 2 * NOPE), BF),
        pltpu.VMEM((SLOTS, keys, 2 * NOPE), BF),
        pltpu.VMEM((2, 2, ROWS, keys), F32),
        pltpu.VMEM((2, 2, ROWS, keys), BF),
        pltpu.VMEM((SLOTS, 2, ROWS, NOPE), F32),
    ]


def first_kernel(
    span_ref, q_nope, q_rope, turned, w_uk, w_uv,
    queries, weights_k, weights_v, acc_out, stats_out,
    q_in, k_in, v_in, sems, lat, ext, *scratch,
):
    copies = [
        pltpu.make_async_copy(source, target, sems.at[i])
        for i, (source, target) in enumerate(((q_nope, q_in), (w_uk, k_in), (w_uv, v_in)))
    ]
    for copy in copies:
        copy.start()
    me = lax.axis_index("ctx")
    cycle = lax.axis_size("ctx")
    prepare_block(span_ref, me, cycle, "own", turned, lat, ext, 0)
    at = lax.broadcasted_iota(jnp.int32, (ROWS, ROPE), 1)
    row = lax.broadcasted_iota(jnp.int32, (ROWS, ROPE), 0)
    which = jnp.where(at == row // HALF, 1.0, 0.0).astype(BF)
    copies[0].wait()
    by_head = jnp.swapaxes(q_in[...], 0, 1)
    for head in range(HEADS):
        queries[head, :, :NOPE] = by_head[head]
        queries[head, :, NOPE:] = jnp.concatenate(
            [q_rope[:, head * ROPE : (head + 1) * ROPE], which], 1
        )
    for copy, source, target in ((copies[1], k_in, weights_k), (copies[2], v_in, weights_v)):
        copy.wait()
        by_head = jnp.swapaxes(source[...], 0, 1)
        for head in range(HEADS):
            target[head // 2, :, (head % 2) * NOPE : (head % 2 + 1) * NOPE] = by_head[head]
    lane = lax.broadcasted_iota(jnp.int32, (ROWS, NOPE), 1)

    def finish(head, top, total, acc):
        acc_out[head] = acc
        held = jnp.where(lane == head, top, total)
        if head == 0:
            stats_out[...] = held
        else:
            keep = (lane != head) & (lane != HEADS + head)
            stats_out[...] = jnp.where(keep, stats_out[...], held)

    attend(
        ROWS, True, lambda p: weights_k[p], lambda p: weights_v[p], queries, lat, ext,
        scratch, None, finish,
    )


def last_kernel(kinds, span_ref, *refs):
    count = len(kinds)
    turned = refs[:count]
    queries, weights_k, weights_v, acc_in, stats_in = refs[count : count + 5]
    attended, log_total, out_heads, log_cols, lat, ext, *scratch = refs[count + 5 :]
    me = lax.axis_index("ctx")
    cycle = lax.axis_size("ctx")
    for n, kind in enumerate(kinds):
        prepare_block(span_ref, me, cycle, kind, turned[n], lat, ext, n * ROWS)
    lane = lax.broadcasted_iota(jnp.int32, (ROWS, NOPE), 1)

    def before(head):
        return (
            stats_in[:, head : head + 1],
            stats_in[:, HEADS + head : HEADS + head + 1],
            acc_in[head],
        )

    def finish(head, top, total, acc):
        out_heads[head] = (acc / total).astype(BF)
        logs = top * SCALE + jnp.log(total)
        log_cols[...] = jnp.where(lane == head, logs, log_cols[...] if head else 0.0)

    attend(
        count * ROWS, False, lambda p: weights_k[p], lambda p: weights_v[p], queries, lat, ext,
        scratch, before, finish,
    )
    attended[...] = jnp.swapaxes(out_heads[...], 0, 1)
    log_total[...] = log_cols[...].T[:HEADS]


HELD = (
    ((HEADS, ROWS, 2 * NOPE), BF),
    ((PAIRS, LATENT, 2 * NOPE), BF),
    ((PAIRS, LATENT, 2 * NOPE), BF),
    ((HEADS, ROWS, NOPE), F32),
    ((ROWS, NOPE), F32),
)


def local(q_nope, q_rope, latent, w_uk, w_uv, span_order):
    turned = latent.T
    kinds = ("mate", "even", "odd", "cross")
    arrived = [exchange(turned, kind) for kind in kinds]
    smem = pl.BlockSpec(memory_space=pltpu.SMEM)
    vmem = pl.BlockSpec(memory_space=pltpu.VMEM)
    hbm = pl.BlockSpec(memory_space=pl.ANY)
    held = pl.pallas_call(
        first_kernel,
        out_shape=[pltpu.VMEM(shape, dtype) for shape, dtype in HELD],
        in_specs=[smem, hbm, vmem, vmem, hbm, hbm],
        out_specs=[vmem] * len(HELD),
        scratch_shapes=[
            pltpu.VMEM((ROWS, HEADS, NOPE), BF),
            pltpu.VMEM((LATENT, HEADS, NOPE), BF),
            pltpu.VMEM((LATENT, HEADS, NOPE), BF),
            pltpu.SemaphoreType.DMA((3,)),
        ]
        + scratch_for(ROWS),
        compiler_params=pltpu.CompilerParams(vmem_limit_bytes=20 << 20),
        cost_estimate=pl.CostEstimate(flops=int(1.7e9), bytes_accessed=15 << 20, transcendentals=1 << 20),
        name="own_block",
    )(span_order, q_nope, q_rope, turned, w_uk, w_uv)
    held = [pltpu.with_memory_space_constraint(x, pltpu.VMEM) for x in held]
    return pl.pallas_call(
        functools.partial(last_kernel, kinds),
        out_shape=[
            jax.ShapeDtypeStruct((ROWS, HEADS, NOPE), BF),
            jax.ShapeDtypeStruct((HEADS, ROWS), F32),
        ],
        in_specs=[smem] + [vmem] * (len(kinds) + len(HELD)),
        out_specs=[vmem, vmem],
        scratch_shapes=[
            pltpu.VMEM((HEADS, ROWS, NOPE), BF),
            pltpu.VMEM((ROWS, NOPE), F32),
        ]
        + scratch_for(len(kinds) * ROWS),
        compiler_params=pltpu.CompilerParams(vmem_limit_bytes=28 << 20),
        cost_estimate=pl.CostEstimate(flops=int(7e9), bytes_accessed=10 << 20, transcendentals=4 << 20),
        name="other_blocks",
    )(span_order, *arrived, *held)


def solution(mesh):
    return jax.shard_map(
        local,
        mesh=mesh,
        in_specs=(
            P("ctx", "head", None),
            P("ctx", "head"),
            P("ctx", None),
            P(None, "head", None),
            P(None, "head", None),
            P(),
        ),
        out_specs=(P("ctx", "head", None), P("head", "ctx")),
        check_vma=False,
    )
```

time: 77.1 us -> 36.3 us (0.47)
  the two profiles are of different devices: /device:TPU:2 before, /device:TPU:1 now
where the time goes in v1:
time: 36.3 us; the launch traced here: 36 us
  Pallas kernels  19.3 us (53%)
  starting transfers between devices  8.91 us (25%)
  local copies, waits for them, and re-layouts  7.07 us (19%)
  between operations  0.7 us (2%)
    pallas_call x1, Pallas kernels, local(): pl.pallas_call(functools.partial(last_kernel, kinds), out_shape=[jax.Shap...  12.7 us
    ppermute x4, starting transfers between devices, exchange(): lax.ppermute(block, 'ctx', [(partner(kind, i, cycle), i) for i in range(c...  8.91 us
    unnamed x14, local copies, waits for them, and re-layouts  7.07 us
    pallas_call x1, Pallas kernels, local(): pl.pallas_call(first_kernel, out_shape=[pltpu.VMEM(shape, dtype) for shap...  6.66 us
  transfers between devices with their start and end apart: 4, of which 0 were waited for; matrix products, arithmetic and copies ran while one was open for 0% of the time, Pallas kernels for 18%

profile of v1, /device:TPU:1, one launch (start us, length us, event | category | flops | bytes accessed | tf_op | source)
XLA Modules:
  0.0 36.0 jit_solution(2243049176826548969)
XLA Ops:
  0.6 0.0 copy-start.6
  0.6 3.1 %collective-permute-start.3 = (bf16[576,256]{1,0:T(8,128)(2,1)}, bf16[576,256]{1,0:T(8,128)(2,1)S(1)}, u32[]{:S(2)}, u32[]{:S(2)}) collective-permute-start(bf16[576,256]{1,0:T(8,128)(2,1)} %bitcast.1), channel_id=1, source_target_pairs={{248,0},{16,8},{8,16},{32,24},{24,32},{48,40},{40,48},{64,56},{56,... | collective-permute-start | bytes 884744 | tf_op jit(solution)/shard_map/ppermute | solution.py:51
  3.8 4.5 %collective-permute-start.2 = (bf16[576,256]{1,0:T(8,128)(2,1)}, bf16[576,256]{1,0:T(8,128)(2,1)S(1)}, u32[]{:S(2)}, u32[]{:S(2)}) collective-permute-start(bf16[576,256]{1,0:T(8,128)(2,1)} %bitcast.2), channel_id=1, source_target_pairs={{240,0},{248,8},{32,16},{40,24},{16,32},{24,40},{64,48},{72,56},{4... | collective-permute-start | bytes 884744 | tf_op jit(solution)/shard_map/ppermute | solution.py:51
  8.2 0.0 collective-permute-start.1
  8.2 1.3 %collective-permute-start = (bf16[576,256]{1,0:T(8,128)(2,1)}, bf16[576,256]{1,0:T(8,128)(2,1)S(1)}, u32[]{:S(2)}, u32[]{:S(2)}) collective-permute-start(bf16[576,256]{1,0:T(8,128)(2,1)} %bitcast.4), channel_id=1, source_target_pairs={{8,0},{0,8},{24,16},{16,24},{40,32},{32,40},{56,48},{48,56},{72,64... | collective-permute-start | bytes 884744 | tf_op jit(solution)/shard_map/ppermute | solution.py:51
  9.6 0.0 copy-start
  9.6 1.6 %copy-done = bf16[512,16,128]{2,1,0:T(8,128)(2,1)S(1)} copy-done((bf16[512,16,128]{2,1,0:T(8,128)(2,1)S(1)}, bf16[512,16,128]{2,1,0:T(8,128)(2,1)}, u32[]{:S(2)}) %copy-start) | copy-done | bytes 2097176
  11.1 0.0 copy-start.1
  11.1 1.6 %copy-done.1 = bf16[512,16,128]{2,1,0:T(8,128)(2,1)S(1)} copy-done((bf16[512,16,128]{2,1,0:T(8,128)(2,1)S(1)}, bf16[512,16,128]{2,1,0:T(8,128)(2,1)}, u32[]{:S(2)}) %copy-start.1) | copy-done | bytes 2097176
  12.7 0.0 copy-start.2
  12.7 1.2 %copy-done.2 = bf16[256,16,128]{2,1,0:T(8,128)(2,1)S(1)} copy-done((bf16[256,16,128]{2,1,0:T(8,128)(2,1)S(1)}, bf16[256,16,128]{2,1,0:T(8,128)(2,1)}, u32[]{:S(2)}) %copy-start.2) | copy-done | bytes 1048600
  14.0 0.0 copy-start.3
  14.0 1.0 %copy-done.3 = bf16[256,1024]{1,0:T(8,128)(2,1)S(1)} copy-done((bf16[256,1024]{1,0:T(8,128)(2,1)S(1)}, bf16[256,1024]{1,0:T(8,128)(2,1)}, u32[]{:S(2)}) %copy-start.3) | copy-done | bytes 524312
  15.0 0.0 copy-start.4
  15.0 1.0 %copy-done.4 = bf16[256,576]{0,1:T(8,128)(2,1)S(1)} copy-done((bf16[256,576]{0,1:T(8,128)(2,1)S(1)}, bf16[256,576]{0,1:T(8,128)(2,1)}, u32[]{:S(2)}) %copy-start.4) | copy-done | bytes 294936
  16.0 0.0 copy-start.5
  16.0 0.7 %copy-done.5 = s32[64]{0:T(128)S(1)} copy-done((s32[64]{0:T(128)S(1)}, s32[64]{0:T(128)}, u32[]{:S(2)}) %copy-start.5) | copy-done | bytes 280
  16.6 6.7 %own_block.1 = (bf16[16,256,256]{2,1,0:T(8,128)(2,1)S(1)}, bf16[8,512,256]{2,1,0:T(8,128)(2,1)S(1)}, bf16[8,512,256]{2,1,0:T(8,128)(2,1)S(1)}, f32[16,256,128]{2,1,0:T(8,128)S(1)}, f32[256,128]{1,0:T(8,128)S(1)}) custom-call(s32[64]{0:T(128)S(1)} %copy-done.5, bf16[256,16,128]{2,1,0:T(8,128)(2,1)S(1)} %copy-done.2, bf16[256,1024]{1,0:T(8,128)(2,1)S(1)} %copy-done.3, ...), custom_call_target="tpu_custom_call" | custom-call | flops 1700000000 | bytes 15728640 | tf_op jit(solution)/shard_map/own_block/pallas_call | solution.py:221
  23.3 0.0 collective-permute-done.3.refs_3_
  23.3 0.0 collective-permute-done.2.refs_2_
  23.3 0.0 collective-permute-done.1.refs_1_
  23.3 0.0 collective-permute-done.refs_0_
  23.3 0.0 copy-done.6
  23.3 12.7 %other_blocks.1 = (bf16[256,16,128]{2,1,0:T(8,128)(2,1)}, f32[16,256]{1,0:T(8,128)}) custom-call(s32[64]{0:T(128)S(1)} %copy-done.6, bf16[576,256]{1,0:T(8,128)(2,1)S(1)} %collective-permute-done.refs_0_, bf16[576,256]{1,0:T(8,128)(2,1)S(1)} %collective-permute-done.1.refs_1_, bf16[576,256]{1,0:T(8,128)(2,1)S(1)} %collective-permute-done.2.refs_2_, ...), custom_call_target="tpu_custom_call" | custom-call | flops 7000000000 | bytes 10485760 | tf_op jit(solution)/shard_map/other_blocks/pallas_call | solution.py:238
Async XLA Ops:
  0.6 22.7 %copy-start.6 = (s32[64]{0:T(128)S(1)}, s32[64]{0:T(128)}, u32[]{:S(2)}) copy-start(s32[64]{0:T(128)} %span_ref.3) | copy-start | bytes 772
  0.6 22.6 %collective-permute-start.3 = (bf16[576,256]{1,0:T(8,128)(2,1)}, bf16[576,256]{1,0:T(8,128)(2,1)S(1)}, u32[]{:S(2)}, u32[]{:S(2)}) collective-permute-start(bf16[576,256]{1,0:T(8,128)(2,1)} %bitcast.1), channel_id=1, source_target_pairs={{248,0},{16,8},{8,16},{32,24},{24,32},{48,40},{40,48},{64,56},{56,... | collective-permute-start | bytes 884744 | tf_op jit(solution)/shard_map/ppermute | solution.py:51
  3.8 19.5 %collective-permute-start.2 = (bf16[576,256]{1,0:T(8,128)(2,1)}, bf16[576,256]{1,0:T(8,128)(2,1)S(1)}, u32[]{:S(2)}, u32[]{:S(2)}) collective-permute-start(bf16[576,256]{1,0:T(8,128)(2,1)} %bitcast.2), channel_id=1, source_target_pairs={{240,0},{248,8},{32,16},{40,24},{16,32},{24,40},{64,48},{72,56},{4... | collective-permute-start | bytes 884744 | tf_op jit(solution)/shard_map/ppermute | solution.py:51
  8.2 15.1 %collective-permute-start.1 = (bf16[576,256]{1,0:T(8,128)(2,1)}, bf16[576,256]{1,0:T(8,128)(2,1)S(1)}, u32[]{:S(2)}, u32[]{:S(2)}) collective-permute-start(bf16[576,256]{1,0:T(8,128)(2,1)} %bitcast.3), channel_id=1, source_target_pairs={{16,0},{24,8},{0,16},{8,24},{48,32},{56,40},{32,48},{40,56},{80,64... | collective-permute-start | bytes 884744 | tf_op jit(solution)/shard_map/ppermute | solution.py:51
  8.2 15.1 %collective-permute-start = (bf16[576,256]{1,0:T(8,128)(2,1)}, bf16[576,256]{1,0:T(8,128)(2,1)S(1)}, u32[]{:S(2)}, u32[]{:S(2)}) collective-permute-start(bf16[576,256]{1,0:T(8,128)(2,1)} %bitcast.4), channel_id=1, source_target_pairs={{8,0},{0,8},{24,16},{16,24},{40,32},{32,40},{56,48},{48,56},{72,64... | collective-permute-start | bytes 884744 | tf_op jit(solution)/shard_map/ppermute | solution.py:51
  9.6 1.6 %copy-start = (bf16[512,16,128]{2,1,0:T(8,128)(2,1)S(1)}, bf16[512,16,128]{2,1,0:T(8,128)(2,1)}, u32[]{:S(2)}) copy-start(bf16[512,16,128]{2,1,0:T(8,128)(2,1)} %w_uk.1) | copy-start | bytes 6291460
  11.1 1.6 %copy-start.1 = (bf16[512,16,128]{2,1,0:T(8,128)(2,1)S(1)}, bf16[512,16,128]{2,1,0:T(8,128)(2,1)}, u32[]{:S(2)}) copy-start(bf16[512,16,128]{2,1,0:T(8,128)(2,1)} %w_uv.1) | copy-start | bytes 6291460
  12.7 1.2 %copy-start.2 = (bf16[256,16,128]{2,1,0:T(8,128)(2,1)S(1)}, bf16[256,16,128]{2,1,0:T(8,128)(2,1)}, u32[]{:S(2)}) copy-start(bf16[256,16,128]{2,1,0:T(8,128)(2,1)} %q_nope.1) | copy-start | bytes 3145732
  14.0 1.0 %copy-start.3 = (bf16[256,1024]{1,0:T(8,128)(2,1)S(1)}, bf16[256,1024]{1,0:T(8,128)(2,1)}, u32[]{:S(2)}) copy-start(bf16[256,1024]{1,0:T(8,128)(2,1)} %q_rope.1) | copy-start | bytes 1572868
  15.0 1.0 %copy-start.4 = (bf16[256,576]{0,1:T(8,128)(2,1)S(1)}, bf16[256,576]{0,1:T(8,128)(2,1)}, u32[]{:S(2)}) copy-start(bf16[256,576]{0,1:T(8,128)(2,1)} %param.8) | copy-start | bytes 884740
  16.0 0.7 %copy-start.5 = (s32[64]{0:T(128)S(1)}, s32[64]{0:T(128)}, u32[]{:S(2)}) copy-start(s32[64]{0:T(128)} %span_ref.3) | copy-start | bytes 772

commit v2 on v1

v2 whole, which is shorter than its diff:
```python
import functools
import math

import jax
import jax.numpy as jnp
from jax import lax
from jax.experimental import pallas as pl
from jax.experimental.pallas import tpu as pltpu
from jax.sharding import PartitionSpec as P

ROWS = 256
HALF = 128
HEADS = 16
NOPE = 128
ROPE = 64
LATENT = 512
PAIRS = HEADS // 2
HIDDEN = -1e30
BF = jnp.bfloat16
F32 = jnp.float32
SCALE = 1.0 / (NOPE + ROPE) ** 0.5
TO_BASE2 = SCALE * math.log2(math.e)
SLOTS = 4
CHUNKS = 4


def dot(a, b):
    return jnp.dot(a, b, preferred_element_type=F32)


def dot_nt(a, b):
    return lax.dot_general(a, b, (((1,), (1,)), ((), ())), preferred_element_type=F32)


def partner(kind, i, cycle):
    chip = i // 2
    if kind == "mate":
        step = 1 - 2 * (i % 2)
    elif kind == "cross":
        step = 2 * (i % 2) - 1
    elif kind == "even":
        step = 2 - 4 * (chip % 2)
    elif kind == "odd":
        step = 4 * (chip % 2) - 2
    else:
        step = 0
    return (i + step + cycle) % cycle


def exchange(block, kind):
    cycle = lax.axis_size("ctx")
    return lax.ppermute(block, "ctx", [(partner(kind, i, cycle), i) for i in range(cycle)])


def visibility(span_ref, me, cycle, kind):
    there = partner(kind, me, cycle)
    lane = lax.broadcasted_iota(jnp.int32, (ROPE, ROWS), 1)
    row = lax.broadcasted_iota(jnp.int32, (ROPE, ROWS), 0)
    span = jnp.where(lane < HALF, span_ref[2 * there], span_ref[2 * there + 1])
    mine = jnp.where(row == 0, span_ref[2 * me], span_ref[2 * me + 1])
    return jnp.where((row < 2) & (span > mine), HIDDEN, 0.0).astype(BF)


def place_block(turned, bias, lat, ext, start):
    lat[start : start + ROWS] = turned[:LATENT].T
    ext[start : start + ROWS] = jnp.concatenate([turned[LATENT:], bias], 0).T


def attend(keys, own, weights_k, weights_v, queries, lat, ext, scratch, before, finish):
    k_buf, v_buf, s_buf, p_buf, m_buf = scratch
    ones = jnp.ones((keys, NOPE), BF)
    if own:
        q_at = lax.broadcasted_iota(jnp.int32, (ROWS, ROWS), 0)
        k_at = lax.broadcasted_iota(jnp.int32, (ROWS, ROWS), 1)
        later = (q_at // HALF == k_at // HALF) & (k_at > q_at)
        own_bias = jnp.where(later, HIDDEN, 0.0).astype(F32)

    def project(pair):
        k_buf[pair % SLOTS] = dot(lat[...], weights_k[pair]).astype(BF)
        v_buf[pair % SLOTS] = dot(lat[...], weights_v[pair]).astype(BF)

    def score(pair):
        for j in range(2):
            head = 2 * pair + j
            part = k_buf[pair % SLOTS, :, j * NOPE : (j + 1) * NOPE]
            scores = dot_nt(queries[head], jnp.concatenate([part, ext[...]], 1))
            if own:
                masked = scores[:, :ROWS] + own_bias
                scores = jnp.concatenate([masked, scores[:, ROWS:]], 1) if keys > ROWS else masked
            s_buf[pair % 2, j] = scores
            top = jnp.broadcast_to(jnp.max(scores, axis=1, keepdims=True), (ROWS, NOPE))
            if before is not None:
                top = jnp.maximum(top, before(head)[0])
            m_buf[pair % SLOTS, j] = top

    def weigh(pair):
        for j in range(2):
            top = m_buf[pair % SLOTS, j]
            for at in range(0, keys, NOPE):
                less = s_buf[pair % 2, j, :, at : at + NOPE] - top
                p_buf[pair % 2, j, :, at : at + NOPE] = jnp.exp2(less * TO_BASE2).astype(BF)

    def combine(pair):
        for j in range(2):
            head = 2 * pair + j
            part = v_buf[pair % SLOTS, :, j * NOPE : (j + 1) * NOPE]
            both = dot(p_buf[pair % 2, j], jnp.concatenate([part, ones], 1))
            total, acc = both[:, NOPE:], both[:, :NOPE]
            top = m_buf[pair % SLOTS, j]
            if before is not None:
                top0, total0, acc0 = before(head)
                fade = jnp.exp2((top0 - top) * TO_BASE2)
                total = total + total0 * fade
                acc = acc + acc0 * fade
            finish(head, top, total, acc)

    for step in range(-2, PAIRS + 1):
        for stage, ahead in ((project, 2), (score, 1), (weigh, 0), (combine, -1)):
            if 0 <= step + ahead < PAIRS:
                stage(step + ahead)


def attend_scratch(keys):
    return [
        pltpu.VMEM((keys, LATENT), BF),
        pltpu.VMEM((keys, NOPE), BF),
        pltpu.VMEM((SLOTS, keys, 2 * NOPE), BF),
        pltpu.VMEM((SLOTS, keys, 2 * NOPE), BF),
        pltpu.VMEM((2, 2, ROWS, keys), F32),
        pltpu.VMEM((2, 2, ROWS, keys), BF),
        pltpu.VMEM((SLOTS, 2, ROWS, NOPE), F32),
    ]


def prepare_kernel(
    spans, q_nope, q_rope, latent, w_uk, w_uv,
    queries, weights_k, weights_v, lat, ext, bias,
    span_ref, turned, q_in, r_in, k_in, v_in, sems,
):
    moves = [(spans, span_ref), (latent, turned), (q_nope, q_in), (q_rope, r_in)]
    chunk = LATENT // CHUNKS
    for source, target in ((w_uk, k_in), (w_uv, v_in)):
        for n in range(CHUNKS):
            rows = pl.ds(n * chunk, chunk)
            moves.append((source.at[rows], target.at[rows]))
    copies = [
        pltpu.make_async_copy(source, target, sems.at[i])
        for i, (source, target) in enumerate(moves)
    ]
    for copy in copies:
        copy.start()
    copies[0].wait()
    copies[1].wait()
    me = lax.axis_index("ctx")
    cycle = lax.axis_size("ctx")
    place_block(turned, visibility(span_ref, me, cycle, "own"), lat, ext, 0)
    for n, kind in enumerate(KINDS):
        bias[n] = visibility(span_ref, me, cycle, kind)
    at = lax.broadcasted_iota(jnp.int32, (ROWS, ROPE), 1)
    row = lax.broadcasted_iota(jnp.int32, (ROWS, ROPE), 0)
    which = jnp.where(at == row // HALF, 1.0, 0.0).astype(BF)
    copies[2].wait()
    copies[3].wait()
    by_head = jnp.swapaxes(q_in[...], 0, 1)
    for head in range(HEADS):
        queries[head, :, :NOPE] = by_head[head]
        queries[head, :, NOPE:] = jnp.concatenate(
            [r_in[:, head * ROPE : (head + 1) * ROPE], which], 1
        )
    for w, (source, target) in enumerate(((k_in, weights_k), (v_in, weights_v))):
        for n in range(CHUNKS):
            copies[4 + w * CHUNKS + n].wait()
            rows = slice(n * chunk, (n + 1) * chunk)
            by_head = jnp.swapaxes(source[rows], 0, 1)
            for head in range(HEADS):
                columns = slice((head % 2) * NOPE, (head % 2 + 1) * NOPE)
                target[head // 2, rows, columns] = by_head[head]


def early_kernel(kinds, queries, weights_k, weights_v, own_lat, own_ext, bias, *refs):
    count = len(kinds)
    blocks, (acc_out, top_out, total_out, lat, ext, *scratch) = refs[:count], refs[count:]
    lat[:ROWS] = own_lat[...]
    ext[:ROWS] = own_ext[...]
    for n, (kind, turned) in enumerate(zip(kinds, blocks)):
        place_block(turned, bias[KINDS.index(kind)], lat, ext, (n + 1) * ROWS)

    def finish(head, top, total, acc):
        acc_out[head] = acc
        top_out[head] = top
        total_out[head] = total

    keys = (count + 1) * ROWS
    attend(keys, True, weights_k, weights_v, queries, lat, ext, scratch, None, finish)


def late_kernel(kinds, queries, weights_k, weights_v, bias, acc_in, top_in, total_in, *refs):
    count = len(kinds)
    blocks, refs = refs[:count], refs[count:]
    attended, log_total, out_heads, tops, totals, lat, ext, *scratch = refs
    for n, (kind, turned) in enumerate(zip(kinds, blocks)):
        place_block(turned, bias[KINDS.index(kind)], lat, ext, n * ROWS)
    lane = lax.broadcasted_iota(jnp.int32, (ROWS, NOPE), 1)

    def before(head):
        return top_in[head], total_in[head], acc_in[head]

    def finish(head, top, total, acc):
        out_heads[head] = (acc / total).astype(BF)
        tops[...] = jnp.where(lane == head, top, tops[...]) if head else top
        totals[...] = jnp.where(lane == head, total, totals[...]) if head else total

    keys = count * ROWS
    attend(keys, False, weights_k, weights_v, queries, lat, ext, scratch, before, finish)
    attended[...] = jnp.swapaxes(out_heads[...], 0, 1)
    log_total[...] = (tops[...] * SCALE + jnp.log(totals[...])).T[:HEADS]


KINDS = ("mate", "even", "odd", "cross")
EARLY = ("mate", "even")
LATE = ("odd", "cross")
STATE = [pltpu.VMEM((HEADS, ROWS, NOPE), F32)] * 3
WHOLE = pl.BlockSpec(memory_space=pltpu.VMEM)
ANYWHERE = pl.BlockSpec(memory_space=pl.ANY)


def params():
    return pltpu.CompilerParams(vmem_limit_bytes=24 << 20)


def cost(blocks):
    return pl.CostEstimate(
        flops=int(1.75e9 * blocks), bytes_accessed=8 << 20, transcendentals=blocks << 20
    )


def in_hbm(*arrays):
    return [pltpu.with_memory_space_constraint(x, pltpu.HBM) for x in arrays]


def in_vmem(*arrays):
    return [pltpu.with_memory_space_constraint(x, pltpu.VMEM) for x in arrays]


def prepare(*inputs):
    outs = [
        pltpu.VMEM((HEADS, ROWS, 2 * NOPE), BF),
        pltpu.VMEM((PAIRS, LATENT, 2 * NOPE), BF),
        pltpu.VMEM((PAIRS, LATENT, 2 * NOPE), BF),
        pltpu.VMEM((ROWS, LATENT), BF),
        pltpu.VMEM((ROWS, NOPE), BF),
        pltpu.VMEM((len(KINDS), ROPE, ROWS), BF),
    ]
    return pl.pallas_call(
        prepare_kernel,
        out_shape=outs,
        in_specs=[ANYWHERE] * 6,
        out_specs=[WHOLE] * len(outs),
        scratch_shapes=[
            pltpu.SMEM((2 * lax.axis_size("ctx"),), jnp.int32),
            pltpu.VMEM((LATENT + ROPE, ROWS), BF),
            pltpu.VMEM((ROWS, HEADS, NOPE), BF),
            pltpu.VMEM((ROWS, HEADS * ROPE), BF),
            pltpu.VMEM((LATENT, HEADS, NOPE), BF),
            pltpu.VMEM((LATENT, HEADS, NOPE), BF),
            pltpu.SemaphoreType.DMA((4 + 2 * CHUNKS,)),
        ],
        compiler_params=params(),
        cost_estimate=cost(1),
        name="prepare",
    )(*in_hbm(*inputs))


def attend_early(prepared, blocks):
    return pl.pallas_call(
        functools.partial(early_kernel, EARLY),
        out_shape=STATE,
        in_specs=[WHOLE] * (len(prepared) + len(blocks)),
        out_specs=[WHOLE] * len(STATE),
        scratch_shapes=attend_scratch((len(EARLY) + 1) * ROWS),
        compiler_params=params(),
        cost_estimate=cost(len(EARLY) + 1),
        name="early_blocks",
    )(*in_vmem(*prepared, *blocks))


def attend_late(prepared, state, blocks):
    queries, weights_k, weights_v, _, _, bias = prepared
    held = (queries, weights_k, weights_v, bias, *state, *blocks)
    return pl.pallas_call(
        functools.partial(late_kernel, LATE),
        out_shape=[
            jax.ShapeDtypeStruct((ROWS, HEADS, NOPE), BF),
            jax.ShapeDtypeStruct((HEADS, ROWS), F32),
        ],
        in_specs=[WHOLE] * len(held),
        out_specs=[WHOLE] * 2,
        scratch_shapes=[
            pltpu.VMEM((HEADS, ROWS, NOPE), BF),
            pltpu.VMEM((ROWS, NOPE), F32),
            pltpu.VMEM((ROWS, NOPE), F32),
        ]
        + attend_scratch(len(LATE) * ROWS),
        compiler_params=params(),
        cost_estimate=cost(len(LATE)),
        name="late_blocks",
    )(*in_vmem(*held))


def local(q_nope, q_rope, latent, w_uk, w_uv, span_order):
    turned = latent.T
    arrived = {kind: exchange(turned, kind) for kind in KINDS}
    prepared = prepare(span_order, q_nope, q_rope, turned, w_uk, w_uv)
    state = attend_early(prepared, [arrived[kind] for kind in EARLY])
    return attend_late(prepared, state, [arrived[kind] for kind in LATE])


def solution(mesh):
    return jax.shard_map(
        local,
        mesh=mesh,
        in_specs=(
            P("ctx", "head", None),
            P("ctx", "head"),
            P("ctx", None),
            P(None, "head", None),
            P(None, "head", None),
            P(),
        ),
        out_specs=(P("ctx", "head", None), P("head", "ctx")),
        check_vma=False,
    )
```

time: 36.3 us -> 27.2 us (0.75)
  local copies, waits for them, and re-layouts: 7.07 us -> 0 us
  Pallas kernels: 19.3 us -> 17.2 us
    unnamed x14 -> x0, local copies, waits for them, and re-layouts: 7.07 us -> none
    pallas_call x2 -> x3, Pallas kernels: 19.3 us -> 17.2 us  [the longest x1 7.48 us: attend_early(): pl.pallas_call(functools.partial(early_kernel, EARLY), out_shape=STATE, i...]
  transfers between devices with their start and end apart: 4 -> 4, of which waited for: 0 -> 0; matrix products, arithmetic and copies ran while one was open for 0% -> 0% of each run, Pallas kernels for 18% -> 41%
where the time goes in v2:
time: 27.2 us; the launch traced here: 27.1 us
  Pallas kernels  17.2 us (63%)
  starting transfers between devices  9.22 us (34%)
  between operations  0.68 us (2%)
    ppermute x4, starting transfers between devices, exchange(): lax.ppermute(block, 'ctx', [(partner(kind, i, cycle), i) for i in range(c...  9.22 us
    pallas_call x1, Pallas kernels, attend_early(): pl.pallas_call(functools.partial(early_kernel, EARLY), out_shape=STATE, i...  7.48 us
    pallas_call x1, Pallas kernels, attend_late(): pl.pallas_call(functools.partial(late_kernel, LATE), out_shape=[jax.Shape...  6.1 us
    pallas_call x1, Pallas kernels, prepare(): pl.pallas_call(prepare_kernel, out_shape=outs, in_specs=[ANYWHERE] * 6, o...  3.63 us
  transfers between devices with their start and end apart: 4, of which 0 were waited for; matrix products, arithmetic and copies ran while one was open for 0% of the time, Pallas kernels for 41%

profile of v2, /device:TPU:1, one launch (start us, length us, event | category | flops | bytes accessed | tf_op | source)
XLA Modules:
  0.0 27.1 jit_solution(15924838975693952584)
XLA Ops:
  0.6 2.6 %collective-permute-start.1 = (bf16[576,256]{1,0:T(8,128)(2,1)}, bf16[576,256]{1,0:T(8,128)(2,1)S(1)}, u32[]{:S(2)}, u32[]{:S(2)}) collective-permute-start(bf16[576,256]{1,0:T(8,128)(2,1)} %bitcast.1), channel_id=1, source_target_pairs={{16,0},{24,8},{0,16},{8,24},{48,32},{56,40},{32,48},{40,56},{80,64... | collective-permute-start | bytes 884744 | tf_op jit(solution)/shard_map/ppermute | solution.py:52
  3.2 1.0 %collective-permute-start = (bf16[576,256]{1,0:T(8,128)(2,1)}, bf16[576,256]{1,0:T(8,128)(2,1)S(1)}, u32[]{:S(2)}, u32[]{:S(2)}) collective-permute-start(bf16[576,256]{1,0:T(8,128)(2,1)} %bitcast.2), channel_id=1, source_target_pairs={{8,0},{0,8},{24,16},{16,24},{40,32},{32,40},{56,48},{48,56},{72,64... | collective-permute-start | bytes 884744 | tf_op jit(solution)/shard_map/ppermute | solution.py:52
  4.1 1.5 %collective-permute-start.3 = (bf16[576,256]{1,0:T(8,128)(2,1)}, bf16[576,256]{1,0:T(8,128)(2,1)S(1)}, u32[]{:S(2)}, u32[]{:S(2)}) collective-permute-start(bf16[576,256]{1,0:T(8,128)(2,1)} %bitcast.3), channel_id=1, source_target_pairs={{248,0},{16,8},{8,16},{32,24},{24,32},{48,40},{40,48},{64,56},{56,... | collective-permute-start | bytes 884744 | tf_op jit(solution)/shard_map/ppermute | solution.py:52
  5.6 4.3 %collective-permute-start.2 = (bf16[576,256]{1,0:T(8,128)(2,1)}, bf16[576,256]{1,0:T(8,128)(2,1)S(1)}, u32[]{:S(2)}, u32[]{:S(2)}) collective-permute-start(bf16[576,256]{1,0:T(8,128)(2,1)} %bitcast.4), channel_id=1, source_target_pairs={{240,0},{248,8},{32,16},{40,24},{16,32},{24,40},{64,48},{72,56},{4... | collective-permute-start | bytes 884744 | tf_op jit(solution)/shard_map/ppermute | solution.py:52
  9.9 3.6 %prepare.1 = (bf16[16,256,256]{2,1,0:T(8,128)(2,1)S(1)}, bf16[8,512,256]{2,1,0:T(8,128)(2,1)S(1)}, bf16[8,512,256]{2,1,0:T(8,128)(2,1)S(1)}, bf16[256,512]{1,0:T...) custom-call(s32[64]{0:T(128)} %spans.1, bf16[256,16,128]{2,1,0:T(8,128)(2,1)} %q_nope.1, ...), custom_call_target="tpu_custom_call" | custom-call | flops 1750000000 | bytes 8388608 | tf_op jit(solution)/shard_map/prepare/pallas_call | solution.py:254
  13.5 0.0 collective-permute-done.1.refs_1_
  13.5 0.0 collective-permute-done.refs_0_
  13.5 7.5 %early_blocks.1 = (f32[16,256,128]{2,1,0:T(8,128)S(1)}, f32[16,256,128]{2,1,0:T(8,128)S(1)}, f32[16,256,128]{2,1,0:T(8,128)S(1)}) custom-call(bf16[16,256,256]{2,1,0:T(8,128)(2,1)S(1)} %get-tuple-element.11.queries, bf16[8,512,256]{2,1,0:T(8,128)(2,1)S(1)} %get-tuple-element.12.weights_k, bf16[8,512,256]{2,1,0:T(8,128)(2,1)S(1)} %get-tuple-element.13.weights_v, ...), custom_call_target="tpu_custom_call" | custom-call | flops 5249999872 | bytes 8388608 | tf_op jit(solution)/shard_map/early_blocks/pallas_call | solution.py:275
  21.0 0.0 collective-permute-done.3.refs_1_
  21.0 0.0 collective-permute-done.2.refs_0_
  21.0 6.1 %late_blocks.1 = (bf16[256,16,128]{2,1,0:T(8,128)(2,1)}, f32[16,256]{1,0:T(8,128)}) custom-call(bf16[16,256,256]{2,1,0:T(8,128)(2,1)S(1)} %get-tuple-element.11.queries, bf16[8,512,256]{2,1,0:T(8,128)(2,1)S(1)} %get-tuple-element.12.weights_k, bf16[8,512,256]{2,1,0:T(8,128)(2,1)S(1)} %get-tuple-element.13.weights_v, ...), custom_call_target="tpu_custom_call" | custom-call | flops 3500000000 | bytes 8388608 | tf_op jit(solution)/shard_map/late_blocks/pallas_call | solution.py:290
Async XLA Ops:
  0.6 12.9 %collective-permute-start.1 = (bf16[576,256]{1,0:T(8,128)(2,1)}, bf16[576,256]{1,0:T(8,128)(2,1)S(1)}, u32[]{:S(2)}, u32[]{:S(2)}) collective-permute-start(bf16[576,256]{1,0:T(8,128)(2,1)} %bitcast.1), channel_id=1, source_target_pairs={{16,0},{24,8},{0,16},{8,24},{48,32},{56,40},{32,48},{40,56},{80,64... | collective-permute-start | bytes 884744 | tf_op jit(solution)/shard_map/ppermute | solution.py:52
  3.2 10.3 %collective-permute-start = (bf16[576,256]{1,0:T(8,128)(2,1)}, bf16[576,256]{1,0:T(8,128)(2,1)S(1)}, u32[]{:S(2)}, u32[]{:S(2)}) collective-permute-start(bf16[576,256]{1,0:T(8,128)(2,1)} %bitcast.2), channel_id=1, source_target_pairs={{8,0},{0,8},{24,16},{16,24},{40,32},{32,40},{56,48},{48,56},{72,64... | collective-permute-start | bytes 884744 | tf_op jit(solution)/shard_map/ppermute | solution.py:52
  4.1 16.9 %collective-permute-start.3 = (bf16[576,256]{1,0:T(8,128)(2,1)}, bf16[576,256]{1,0:T(8,128)(2,1)S(1)}, u32[]{:S(2)}, u32[]{:S(2)}) collective-permute-start(bf16[576,256]{1,0:T(8,128)(2,1)} %bitcast.3), channel_id=1, source_target_pairs={{248,0},{16,8},{8,16},{32,24},{24,32},{48,40},{40,48},{64,56},{56,... | collective-permute-start | bytes 884744 | tf_op jit(solution)/shard_map/ppermute | solution.py:52
  5.6 15.4 %collective-permute-start.2 = (bf16[576,256]{1,0:T(8,128)(2,1)}, bf16[576,256]{1,0:T(8,128)(2,1)S(1)}, u32[]{:S(2)}, u32[]{:S(2)}) collective-permute-start(bf16[576,256]{1,0:T(8,128)(2,1)} %bitcast.4), channel_id=1, source_target_pairs={{240,0},{248,8},{32,16},{40,24},{16,32},{24,40},{64,48},{72,56},{4... | collective-permute-start | bytes 884744 | tf_op jit(solution)/shard_map/ppermute | solution.py:52

commit v3 on v2

--- a/solution.py
+++ b/solution.py
@@ -47,9 +47,10 @@
     return (i + step + cycle) % cycle
 
 
-def exchange(block, kind):
+def exchange(block, kind, held_by_mate=False):
     cycle = lax.axis_size("ctx")
-    return lax.ppermute(block, "ctx", [(partner(kind, i, cycle), i) for i in range(cycle)])
+    pairs = [(partner(kind, i, cycle) ^ held_by_mate, i) for i in range(cycle)]
+    return lax.ppermute(block, "ctx", pairs)
 
 
 def visibility(span_ref, me, cycle, kind):
@@ -132,49 +133,36 @@
     ]
 
 
+def hand_on_kernel(block, out, which):
+    at = lax.broadcasted_iota(jnp.int32, (ROWS, ROPE), 1)
+    row = lax.broadcasted_iota(jnp.int32, (ROWS, ROPE), 0)
+    which[...] = jnp.where(at == row // HALF, 1.0, 0.0).astype(BF)
+
+
 def prepare_kernel(
-    spans, q_nope, q_rope, latent, w_uk, w_uv,
+    spans, q_nope, q_rope, turned, w_uk, w_uv, which,
     queries, weights_k, weights_v, lat, ext, bias,
-    span_ref, turned, q_in, r_in, k_in, v_in, sems,
+    span_ref, sem,
 ):
-    moves = [(spans, span_ref), (latent, turned), (q_nope, q_in), (q_rope, r_in)]
-    chunk = LATENT // CHUNKS
-    for source, target in ((w_uk, k_in), (w_uv, v_in)):
-        for n in range(CHUNKS):
-            rows = pl.ds(n * chunk, chunk)
-            moves.append((source.at[rows], target.at[rows]))
-    copies = [
-        pltpu.make_async_copy(source, target, sems.at[i])
-        for i, (source, target) in enumerate(moves)
-    ]
-    for copy in copies:
-        copy.start()
-    copies[0].wait()
-    copies[1].wait()
+    copy = pltpu.make_async_copy(spans, span_ref, sem)
+    copy.start()
+    by_head = jnp.swapaxes(q_nope[...], 0, 1)
+    for head in range(HEADS):
+        queries[head, :, :NOPE] = by_head[head]
+        queries[head, :, NOPE:] = jnp.concatenate(
+            [q_rope[:, head * ROPE : (head + 1) * ROPE], which[...]], 1
+        )
+    for source, target in ((w_uk, weights_k), (w_uv, weights_v)):
+        by_head = jnp.swapaxes(source[...], 0, 1)
+        for head in range(HEADS):
+            columns = slice((head % 2) * NOPE, (head % 2 + 1) * NOPE)
+            target[head // 2, :, columns] = by_head[head]
+    copy.wait()
     me = lax.axis_index("ctx")
     cycle = lax.axis_size("ctx")
     place_block(turned, visibility(span_ref, me, cycle, "own"), lat, ext, 0)
     for n, kind in enumerate(KINDS):
         bias[n] = visibility(span_ref, me, cycle, kind)
-    at = lax.broadcasted_iota(jnp.int32, (ROWS, ROPE), 1)
-    row = lax.broadcasted_iota(jnp.int32, (ROWS, ROPE), 0)
-    which = jnp.where(at == row // HALF, 1.0, 0.0).astype(BF)
-    copies[2].wait()
-    copies[3].wait()
-    by_head = jnp.swapaxes(q_in[...], 0, 1)
-    for head in range(HEADS):
-        queries[head, :, :NOPE] = by_head[head]
-        queries[head, :, NOPE:] = jnp.concatenate(
-            [r_in[:, head * ROPE : (head + 1) * ROPE], which], 1
-        )
-    for w, (source, target) in enumerate(((k_in, weights_k), (v_in, weights_v))):
-        for n in range(CHUNKS):
-            copies[4 + w * CHUNKS + n].wait()
-            rows = slice(n * chunk, (n + 1) * chunk)
-            by_head = jnp.swapaxes(source[rows], 0, 1)
-            for head in range(HEADS):
-                columns = slice((head % 2) * NOPE, (head % 2 + 1) * NOPE)
-                target[head // 2, rows, columns] = by_head[head]
 
 
 def early_kernel(kinds, queries, weights_k, weights_v, own_lat, own_ext, bias, *refs):
@@ -218,7 +206,7 @@
 
 KINDS = ("mate", "even", "odd", "cross")
 EARLY = ("mate", "even")
-LATE = ("odd", "cross")
+LATE = ("cross", "odd")
 STATE = [pltpu.VMEM((HEADS, ROWS, NOPE), F32)] * 3
 WHOLE = pl.BlockSpec(memory_space=pltpu.VMEM)
 ANYWHERE = pl.BlockSpec(memory_space=pl.ANY)
@@ -242,7 +230,7 @@
     return [pltpu.with_memory_space_constraint(x, pltpu.VMEM) for x in arrays]
 
 
-def prepare(*inputs):
+def prepare(spans, *inputs):
     outs = [
         pltpu.VMEM((HEADS, ROWS, 2 * NOPE), BF),
         pltpu.VMEM((PAIRS, LATENT, 2 * NOPE), BF),
@@ -254,21 +242,29 @@
     return pl.pallas_call(
         prepare_kernel,
         out_shape=outs,
-        in_specs=[ANYWHERE] * 6,
+        in_specs=[ANYWHERE] + [WHOLE] * 6,
         out_specs=[WHOLE] * len(outs),
         scratch_shapes=[
             pltpu.SMEM((2 * lax.axis_size("ctx"),), jnp.int32),
-            pltpu.VMEM((LATENT + ROPE, ROWS), BF),
-            pltpu.VMEM((ROWS, HEADS, NOPE), BF),
-            pltpu.VMEM((ROWS, HEADS * ROPE), BF),
-            pltpu.VMEM((LATENT, HEADS, NOPE), BF),
-            pltpu.VMEM((LATENT, HEADS, NOPE), BF),
-            pltpu.SemaphoreType.DMA((4 + 2 * CHUNKS,)),
+            pltpu.SemaphoreType.DMA,
         ],
         compiler_params=params(),
         cost_estimate=cost(1),
         name="prepare",
-    )(*in_hbm(*inputs))
+    )(*in_hbm(spans), *in_vmem(*inputs))
+
+
+def hand_on(block):
+    return pl.pallas_call(
+        hand_on_kernel,
+        out_shape=[pltpu.VMEM((LATENT + ROPE, ROWS), BF), pltpu.VMEM((ROWS, ROPE), BF)],
+        in_specs=[WHOLE],
+        out_specs=[WHOLE] * 2,
+        input_output_aliases={0: 0},
+        compiler_params=pltpu.CompilerParams(vmem_limit_bytes=4 << 20),
+        cost_estimate=cost(8),
+        name="hand_on",
+    )(*in_vmem(block))
 
 
 def attend_early(prepared, blocks):
@@ -309,8 +305,10 @@
 
 def local(q_nope, q_rope, latent, w_uk, w_uv, span_order):
     turned = latent.T
-    arrived = {kind: exchange(turned, kind) for kind in KINDS}
-    prepared = prepare(span_order, q_nope, q_rope, turned, w_uk, w_uv)
+    arrived = {kind: exchange(turned, kind) for kind in EARLY}
+    arrived["mate"], which = hand_on(arrived["mate"])
+    arrived |= {kind: exchange(arrived["mate"], kind, held_by_mate=True) for kind in LATE}
+    prepared = prepare(span_order, q_nope, q_rope, turned, w_uk, w_uv, which)
     state = attend_early(prepared, [arrived[kind] for kind in EARLY])
     return attend_late(prepared, state, [arrived[kind] for kind in LATE])
 

time: 27.2 us -> 26.8 us (0.985)
  waiting for transfers between devices: 0.01 us -> 1.51 us
  Pallas kernels: 17.2 us -> 15.9 us
  starting transfers between devices: 9.22 us -> 8.56 us
    ppermute x4, waiting for transfers between devices: 0.01 us -> 1.51 us  [exchange(): return lax.ppermute(block, 'ctx', pairs)]
    pallas_call x1 -> x2, Pallas kernels: 3.63 us -> 2.36 us  [the longest x1 2.33 us: prepare(): pl.pallas_call(prepare_kernel, out_shape=outs, in_specs=[ANYWHERE] + [WHO...]
    ppermute x4, starting transfers between devices: 9.22 us -> 8.56 us  [exchange(): return lax.ppermute(block, 'ctx', pairs)]
  transfers between devices with their start and end apart: 4 -> 4, of which waited for: 0 -> 2; matrix products, arithmetic and copies ran while one was open for 0% -> 0% of each run, Pallas kernels for 41% -> 37%
where the time goes in v3:
time: 26.8 us
  Pallas kernels  15.9 us (59%)
  starting transfers between devices  8.56 us (32%)
  waiting for transfers between devices  1.51 us (6%)
  between operations  0.72 us (3%)
    ppermute x4, starting transfers between devices, exchange(): return lax.ppermute(block, 'ctx', pairs)  8.56 us
    pallas_call x1, Pallas kernels, attend_early(): pl.pallas_call(functools.partial(early_kernel, EARLY), out_shape=STATE, i...  7.47 us
    pallas_call x1, Pallas kernels, attend_late(): pl.pallas_call(functools.partial(late_kernel, LATE), out_shape=[jax.Shape...  6.11 us
    pallas_call x1, Pallas kernels, prepare(): pl.pallas_call(prepare_kernel, out_shape=outs, in_specs=[ANYWHERE] + [WHO...  2.33 us
    ppermute x4, waiting for transfers between devices, exchange(): return lax.ppermute(block, 'ctx', pairs)  1.51 us
  transfers between devices with their start and end apart: 4, of which 2 were waited for; matrix products, arithmetic and copies ran while one was open for 0% of the time, Pallas kernels for 37%

profile of v3, /device:TPU:1, one launch (start us, length us, event | category | flops | bytes accessed | tf_op | source)
XLA Modules:
  0.0 26.8 jit_solution(1295152848531394160)
XLA Ops:
  0.6 0.0 copy-start
  0.6 0.0 copy-start.1
  0.7 0.0 copy-start.2
  0.7 0.0 copy-start.3
  0.7 0.0 copy-start.4
  0.7 3.3 %collective-permute-start = (bf16[576,256]{1,0:T(8,128)(2,1)}, bf16[576,256]{1,0:T(8,128)(2,1)S(1)}, u32[]{:S(2)}, u32[]{:S(2)}) collective-permute-start(bf16[576,256]{1,0:T(8,128)(2,1)} %bitcast.1), channel_id=1, source_target_pairs={{8,0},{0,8},{24,16},{16,24},{40,32},{32,40},{56,48},{48,56},{72,64... | collective-permute-start | bytes 884744 | tf_op jit(solution)/shard_map/ppermute | solution.py:53
  4.0 0.0 collective-permute-start.1
  4.0 1.4 %collective-permute-done.block = bf16[576,256]{1,0:T(8,128)(2,1)S(1)} collective-permute-done((bf16[576,256]{1,0:T(8,128)(2,1)}, bf16[576,256]{1,0:T(8,128)(2,1)S(1)}, u32[]{:S(2)}, u32[]{:S(2)}) %collective-permute-start) | collective-permute-done | bytes 294944 | tf_op jit(solution)/shard_map/ppermute | solution.py:53
  5.5 5.2 %collective-permute-start.3 = (bf16[576,256]{1,0:T(8,128)(2,1)S(1)}, bf16[576,256]{1,0:T(8,128)(2,1)S(1)}, u32[]{:S(2)}, u32[]{:S(2)}) collective-permute-start(bf16[576,256]{1,0:T(8,128)(2,1)S(1)} %get-tuple-element.20.refs_0_), channel_id=1, source_target_pairs={{248,0},{240,8},{40,16},{32,24},{24,32},{16,40},{72,48},{64,56},{5... | collective-permute-start | bytes 884744 | tf_op jit(solution)/shard_map/ppermute | solution.py:53
  10.7 0.0 collective-permute-start.2
  10.7 0.0 copy-done
  10.7 0.0 copy-done.1
  10.7 0.0 copy-done.2
  10.7 0.0 copy-done.3
  10.7 0.0 copy-done.4
  10.7 2.3 %prepare.1 = (bf16[16,256,256]{2,1,0:T(8,128)(2,1)S(1)}, bf16[8,512,256]{2,1,0:T(8,128)(2,1)S(1)}, bf16[8,512,256]{2,1,0:T(8,128)(2,1)S(1)}, bf16[256,512]{1,0:T...) custom-call(s32[64]{0:T(128)} %spans.1, bf16[256,16,128]{2,1,0:T(8,128)(2,1)S(1)} %copy-done.2, ...), custom_call_target="tpu_custom_call" | custom-call | flops 1750000000 | bytes 8388608 | tf_op jit(solution)/shard_map/prepare/pallas_call | solution.py:242
  13.1 0.0 collective-permute-done.1.refs_1_
  13.1 7.5 %early_blocks.1 = (f32[16,256,128]{2,1,0:T(8,128)S(1)}, f32[16,256,128]{2,1,0:T(8,128)S(1)}, f32[16,256,128]{2,1,0:T(8,128)S(1)}) custom-call(bf16[16,256,256]{2,1,0:T(8,128)(2,1)S(1)} %get-tuple-element.14.queries, bf16[8,512,256]{2,1,0:T(8,128)(2,1)S(1)} %get-tuple-element.15.weights_k, bf16[8,512,256]{2,1,0:T(8,128)(2,1)S(1)} %get-tuple-element.16.weights_v, ...), custom_call_target="tpu_custom_call" | custom-call | flops 5249999872 | bytes 8388608 | tf_op jit(solution)/shard_map/early_blocks/pallas_call | solution.py:271
  20.5 0.0 collective-permute-done.3.refs_1_
  20.6 0.1 collective-permute-done.2.refs_0_
  20.6 6.1 %late_blocks.1 = (bf16[256,16,128]{2,1,0:T(8,128)(2,1)}, f32[16,256]{1,0:T(8,128)}) custom-call(bf16[16,256,256]{2,1,0:T(8,128)(2,1)S(1)} %get-tuple-element.14.queries, bf16[8,512,256]{2,1,0:T(8,128)(2,1)S(1)} %get-tuple-element.15.weights_k, bf16[8,512,256]{2,1,0:T(8,128)(2,1)S(1)} %get-tuple-element.16.weights_v, ...), custom_call_target="tpu_custom_call" | custom-call | flops 3500000000 | bytes 8388608 | tf_op jit(solution)/shard_map/late_blocks/pallas_call | solution.py:286
  (1 shorter events, 0.0 us)
Async XLA Ops:
  0.6 10.1 %copy-start = (bf16[512,16,128]{2,1,0:T(8,128)(2,1)S(1)}, bf16[512,16,128]{2,1,0:T(8,128)(2,1)}, u32[]{:S(2)}) copy-start(bf16[512,16,128]{2,1,0:T(8,128)(2,1)} %w_uk.1) | copy-start | bytes 6291460
  0.6 10.1 %copy-start.1 = (bf16[512,16,128]{2,1,0:T(8,128)(2,1)S(1)}, bf16[512,16,128]{2,1,0:T(8,128)(2,1)}, u32[]{:S(2)}) copy-start(bf16[512,16,128]{2,1,0:T(8,128)(2,1)} %w_uv.1) | copy-start | bytes 6291460
  0.7 10.0 %copy-start.2 = (bf16[256,16,128]{2,1,0:T(8,128)(2,1)S(1)}, bf16[256,16,128]{2,1,0:T(8,128)(2,1)}, u32[]{:S(2)}) copy-start(bf16[256,16,128]{2,1,0:T(8,128)(2,1)} %q_nope.1) | copy-start | bytes 3145732
  0.7 10.0 %copy-start.3 = (bf16[256,1024]{1,0:T(8,128)(2,1)S(1)}, bf16[256,1024]{1,0:T(8,128)(2,1)}, u32[]{:S(2)}) copy-start(bf16[256,1024]{1,0:T(8,128)(2,1)} %q_rope.1) | copy-start | bytes 1572868
  0.7 10.0 %copy-start.4 = (bf16[256,576]{0,1:T(8,128)(2,1)S(1)}, bf16[256,576]{0,1:T(8,128)(2,1)}, u32[]{:S(2)}) copy-start(bf16[256,576]{0,1:T(8,128)(2,1)} %param.8) | copy-start | bytes 884740
  0.7 4.7 %collective-permute-start = (bf16[576,256]{1,0:T(8,128)(2,1)}, bf16[576,256]{1,0:T(8,128)(2,1)S(1)}, u32[]{:S(2)}, u32[]{:S(2)}) collective-permute-start(bf16[576,256]{1,0:T(8,128)(2,1)} %bitcast.1), channel_id=1, source_target_pairs={{8,0},{0,8},{24,16},{16,24},{40,32},{32,40},{56,48},{48,56},{72,64... | collective-permute-start | bytes 884744 | tf_op jit(solution)/shard_map/ppermute | solution.py:53
  4.0 9.1 %collective-permute-start.1 = (bf16[576,256]{1,0:T(8,128)(2,1)}, bf16[576,256]{1,0:T(8,128)(2,1)S(1)}, u32[]{:S(2)}, u32[]{:S(2)}) collective-permute-start(bf16[576,256]{1,0:T(8,128)(2,1)} %bitcast.2), channel_id=1, source_target_pairs={{16,0},{24,8},{0,16},{8,24},{48,32},{56,40},{32,48},{40,56},{80,64... | collective-permute-start | bytes 884744 | tf_op jit(solution)/shard_map/ppermute | solution.py:53
  5.5 15.1 %collective-permute-start.3 = (bf16[576,256]{1,0:T(8,128)(2,1)S(1)}, bf16[576,256]{1,0:T(8,128)(2,1)S(1)}, u32[]{:S(2)}, u32[]{:S(2)}) collective-permute-start(bf16[576,256]{1,0:T(8,128)(2,1)S(1)} %get-tuple-element.20.refs_0_), channel_id=1, source_target_pairs={{248,0},{240,8},{40,16},{32,24},{24,32},{16,40},{72,48},{64,56},{5... | collective-permute-start | bytes 884744 | tf_op jit(solution)/shard_map/ppermute | solution.py:53
  10.7 10.0 %collective-permute-start.2 = (bf16[576,256]{1,0:T(8,128)(2,1)S(1)}, bf16[576,256]{1,0:T(8,128)(2,1)S(1)}, u32[]{:S(2)}, u32[]{:S(2)}) collective-permute-start(bf16[576,256]{1,0:T(8,128)(2,1)S(1)} %get-tuple-element.20.refs_0_), channel_id=1, source_target_pairs={{240,0},{24,8},{0,16},{40,24},{16,32},{56,40},{32,48},{72,56},{48,... | collective-permute-start | bytes 884744 | tf_op jit(solution)/shard_map/ppermute | solution.py:53

commit v4 on v3

--- a/solution.py
+++ b/solution.py
@@ -47,10 +47,9 @@
     return (i + step + cycle) % cycle
 
 
-def exchange(block, kind, held_by_mate=False):
+def exchange(block, kind):
     cycle = lax.axis_size("ctx")
-    pairs = [(partner(kind, i, cycle) ^ held_by_mate, i) for i in range(cycle)]
-    return lax.ppermute(block, "ctx", pairs)
+    return lax.ppermute(block, "ctx", [(partner(kind, i, cycle), i) for i in range(cycle)])
 
 
 def visibility(span_ref, me, cycle, kind):
@@ -133,7 +132,7 @@
     ]
 
 
-def hand_on_kernel(block, out, which):
+def mark_kernel(which):
     at = lax.broadcasted_iota(jnp.int32, (ROWS, ROPE), 1)
     row = lax.broadcasted_iota(jnp.int32, (ROWS, ROPE), 0)
     which[...] = jnp.where(at == row // HALF, 1.0, 0.0).astype(BF)
@@ -182,9 +181,10 @@
     attend(keys, True, weights_k, weights_v, queries, lat, ext, scratch, None, finish)
 
 
-def late_kernel(kinds, queries, weights_k, weights_v, bias, acc_in, top_in, total_in, *refs):
+def late_kernel(kinds, *refs):
     count = len(kinds)
     blocks, refs = refs[:count], refs[count:]
+    queries, weights_k, weights_v, bias, acc_in, top_in, total_in, *refs = refs
     attended, log_total, out_heads, tops, totals, lat, ext, *scratch = refs
     for n, (kind, turned) in enumerate(zip(kinds, blocks)):
         place_block(turned, bias[KINDS.index(kind)], lat, ext, n * ROWS)
@@ -206,7 +206,7 @@
 
 KINDS = ("mate", "even", "odd", "cross")
 EARLY = ("mate", "even")
-LATE = ("cross", "odd")
+LATE = ("odd", "cross")
 STATE = [pltpu.VMEM((HEADS, ROWS, NOPE), F32)] * 3
 WHOLE = pl.BlockSpec(memory_space=pltpu.VMEM)
 ANYWHERE = pl.BlockSpec(memory_space=pl.ANY)
@@ -254,17 +254,15 @@
     )(*in_hbm(spans), *in_vmem(*inputs))
 
 
-def hand_on(block):
+def mark_slots():
     return pl.pallas_call(
-        hand_on_kernel,
-        out_shape=[pltpu.VMEM((LATENT + ROPE, ROWS), BF), pltpu.VMEM((ROWS, ROPE), BF)],
-        in_specs=[WHOLE],
-        out_specs=[WHOLE] * 2,
-        input_output_aliases={0: 0},
+        mark_kernel,
+        out_shape=pltpu.VMEM((ROWS, ROPE), BF),
+        out_specs=WHOLE,
         compiler_params=pltpu.CompilerParams(vmem_limit_bytes=4 << 20),
         cost_estimate=cost(8),
-        name="hand_on",
-    )(*in_vmem(block))
+        name="mark_slots",
+    )()
 
 
 def attend_early(prepared, blocks):
@@ -282,7 +280,7 @@
 
 def attend_late(prepared, state, blocks):
     queries, weights_k, weights_v, _, _, bias = prepared
-    held = (queries, weights_k, weights_v, bias, *state, *blocks)
+    held = (*blocks, queries, weights_k, weights_v, bias, *state)
     return pl.pallas_call(
         functools.partial(late_kernel, LATE),
         out_shape=[
@@ -305,9 +303,8 @@
 
 def local(q_nope, q_rope, latent, w_uk, w_uv, span_order):
     turned = latent.T
-    arrived = {kind: exchange(turned, kind) for kind in EARLY}
-    arrived["mate"], which = hand_on(arrived["mate"])
-    arrived |= {kind: exchange(arrived["mate"], kind, held_by_mate=True) for kind in LATE}
+    arrived = {kind: exchange(turned, kind) for kind in KINDS}
+    which = mark_slots()
     prepared = prepare(span_order, q_nope, q_rope, turned, w_uk, w_uv, which)
     state = attend_early(prepared, [arrived[kind] for kind in EARLY])
     return attend_late(prepared, state, [arrived[kind] for kind in LATE])

time: 26.8 us -> 26 us (0.970)
  waiting for transfers between devices: 1.51 us -> 0.01 us
  starting transfers between devices: 8.56 us -> 9.22 us
    ppermute x4, waiting for transfers between devices: 1.51 us -> 0.01 us  [exchange(): lax.ppermute(block, 'ctx', [(partner(kind, i, cycle), i) for i in range(c...]
    ppermute x4, starting transfers between devices: 8.56 us -> 9.22 us  [exchange(): lax.ppermute(block, 'ctx', [(partner(kind, i, cycle), i) for i in range(c...]
  transfers between devices with their start and end apart: 4 -> 4, of which waited for: 2 -> 0; matrix products, arithmetic and copies ran while one was open for 0% -> 0% of each run, Pallas kernels for 37% -> 38%
where the time goes in v4:
time: 26 us; the launch traced here: 25.9 us
  Pallas kernels  15.9 us (61%)
  starting transfers between devices  9.22 us (35%)
  between operations  0.76 us (3%)
    ppermute x4, starting transfers between devices, exchange(): lax.ppermute(block, 'ctx', [(partner(kind, i, cycle), i) for i in range(c...  9.22 us
    pallas_call x1, Pallas kernels, attend_early(): pl.pallas_call(functools.partial(early_kernel, EARLY), out_shape=STATE, i...  7.47 us
    pallas_call x1, Pallas kernels, attend_late(): pl.pallas_call(functools.partial(late_kernel, LATE), out_shape=[jax.Shape...  6.11 us
    pallas_call x1, Pallas kernels, prepare(): pl.pallas_call(prepare_kernel, out_shape=outs, in_specs=[ANYWHERE] + [WHO...  2.32 us
  transfers between devices with their start and end apart: 4, of which 0 were waited for; matrix products, arithmetic and copies ran while one was open for 0% of the time, Pallas kernels for 38%

profile of v4, /device:TPU:1, one launch (start us, length us, event | category | flops | bytes accessed | tf_op | source)
XLA Modules:
  0.0 25.9 jit_solution(11935954913050796595)
XLA Ops:
  0.6 0.0 copy-start
  0.6 0.0 copy-start.1
  0.7 0.0 copy-start.2
  0.7 0.0 copy-start.3
  0.7 0.0 copy-start.4
  0.7 2.6 %collective-permute-start.3 = (bf16[576,256]{1,0:T(8,128)(2,1)}, bf16[576,256]{1,0:T(8,128)(2,1)S(1)}, u32[]{:S(2)}, u32[]{:S(2)}) collective-permute-start(bf16[576,256]{1,0:T(8,128)(2,1)} %bitcast.1), channel_id=1, source_target_pairs={{16,0},{24,8},{0,16},{8,24},{48,32},{56,40},{32,48},{40,56},{80,64... | collective-permute-start | bytes 884744 | tf_op jit(solution)/shard_map/ppermute | solution.py:52
  3.2 1.0 %collective-permute-start.2 = (bf16[576,256]{1,0:T(8,128)(2,1)}, bf16[576,256]{1,0:T(8,128)(2,1)S(1)}, u32[]{:S(2)}, u32[]{:S(2)}) collective-permute-start(bf16[576,256]{1,0:T(8,128)(2,1)} %bitcast.2), channel_id=1, source_target_pairs={{8,0},{0,8},{24,16},{16,24},{40,32},{32,40},{56,48},{48,56},{72,64... | collective-permute-start | bytes 884744 | tf_op jit(solution)/shard_map/ppermute | solution.py:52
  4.2 1.5 %collective-permute-start.1 = (bf16[576,256]{1,0:T(8,128)(2,1)}, bf16[576,256]{1,0:T(8,128)(2,1)S(1)}, u32[]{:S(2)}, u32[]{:S(2)}) collective-permute-start(bf16[576,256]{1,0:T(8,128)(2,1)} %bitcast.3), channel_id=1, source_target_pairs={{248,0},{16,8},{8,16},{32,24},{24,32},{48,40},{40,48},{64,56},{56,... | collective-permute-start | bytes 884744 | tf_op jit(solution)/shard_map/ppermute | solution.py:52
  5.6 4.3 %collective-permute-start = (bf16[576,256]{1,0:T(8,128)(2,1)}, bf16[576,256]{1,0:T(8,128)(2,1)S(1)}, u32[]{:S(2)}, u32[]{:S(2)}) collective-permute-start(bf16[576,256]{1,0:T(8,128)(2,1)} %bitcast.4), channel_id=1, source_target_pairs={{240,0},{248,8},{32,16},{40,24},{16,32},{24,40},{64,48},{72,56},{4... | collective-permute-start | bytes 884744 | tf_op jit(solution)/shard_map/ppermute | solution.py:52
  9.9 0.0 copy-done
  9.9 0.0 copy-done.1
  10.0 0.0 copy-done.2
  10.0 0.0 copy-done.3
  10.0 0.0 copy-done.4
  10.0 2.3 %prepare.1 = (bf16[16,256,256]{2,1,0:T(8,128)(2,1)S(1)}, bf16[8,512,256]{2,1,0:T(8,128)(2,1)S(1)}, bf16[8,512,256]{2,1,0:T(8,128)(2,1)S(1)}, bf16[256,512]{1,0:T...) custom-call(s32[64]{0:T(128)} %spans.1, bf16[256,16,128]{2,1,0:T(8,128)(2,1)S(1)} %copy-done.2, ...), custom_call_target="tpu_custom_call" | custom-call | flops 1750000000 | bytes 8388608 | tf_op jit(solution)/shard_map/prepare/pallas_call | solution.py:242
  12.3 0.0 collective-permute-done.3.refs_1_
  12.3 0.0 collective-permute-done.2.refs_0_
  12.3 7.5 %early_blocks.1 = (f32[16,256,128]{2,1,0:T(8,128)S(1)}, f32[16,256,128]{2,1,0:T(8,128)S(1)}, f32[16,256,128]{2,1,0:T(8,128)S(1)}) custom-call(bf16[16,256,256]{2,1,0:T(8,128)(2,1)S(1)} %get-tuple-element.11.queries.refs_2_, bf16[8,512,256]{2,1,0:T(8,128)(2,1)S(1)} %get-tuple-element.12.weights_k.refs_3_, ...), custom_call_target="tpu_custom_call" | custom-call | flops 5249999872 | bytes 8388608 | tf_op jit(solution)/shard_map/early_blocks/pallas_call | solution.py:269
  19.8 0.0 collective-permute-done.1.refs_1_
  19.8 0.0 collective-permute-done.refs_0_
  19.8 6.1 %late_blocks.1 = (bf16[256,16,128]{2,1,0:T(8,128)(2,1)}, f32[16,256]{1,0:T(8,128)}) custom-call(bf16[576,256]{1,0:T(8,128)(2,1)S(1)} %collective-permute-done.refs_0_, bf16[576,256]{1,0:T(8,128)(2,1)S(1)} %collective-permute-done.1.refs_1_, bf16[16,256,256]{2,1,0:T(8,128)(2,1)S(1)} %get-tuple-element.11.queries.refs_2_, ...), custom_call_target="tpu_custom_call" | custom-call | flops 3500000000 | bytes 8388608 | tf_op jit(solution)/shard_map/late_blocks/pallas_call | solution.py:284
  (1 shorter events, 0.0 us)
Async XLA Ops:
  0.6 9.3 %copy-start = (bf16[512,16,128]{2,1,0:T(8,128)(2,1)S(1)}, bf16[512,16,128]{2,1,0:T(8,128)(2,1)}, u32[]{:S(2)}) copy-start(bf16[512,16,128]{2,1,0:T(8,128)(2,1)} %w_uk.1) | copy-start | bytes 6291460
  0.6 9.3 %copy-start.1 = (bf16[512,16,128]{2,1,0:T(8,128)(2,1)S(1)}, bf16[512,16,128]{2,1,0:T(8,128)(2,1)}, u32[]{:S(2)}) copy-start(bf16[512,16,128]{2,1,0:T(8,128)(2,1)} %w_uv.1) | copy-start | bytes 6291460
  0.7 9.3 %copy-start.2 = (bf16[256,16,128]{2,1,0:T(8,128)(2,1)S(1)}, bf16[256,16,128]{2,1,0:T(8,128)(2,1)}, u32[]{:S(2)}) copy-start(bf16[256,16,128]{2,1,0:T(8,128)(2,1)} %q_nope.1) | copy-start | bytes 3145732
  0.7 9.3 %copy-start.3 = (bf16[256,1024]{1,0:T(8,128)(2,1)S(1)}, bf16[256,1024]{1,0:T(8,128)(2,1)}, u32[]{:S(2)}) copy-start(bf16[256,1024]{1,0:T(8,128)(2,1)} %q_rope.1) | copy-start | bytes 1572868
  0.7 9.3 %copy-start.4 = (bf16[256,576]{0,1:T(8,128)(2,1)S(1)}, bf16[256,576]{0,1:T(8,128)(2,1)}, u32[]{:S(2)}) copy-start(bf16[256,576]{0,1:T(8,128)(2,1)} %param.8) | copy-start | bytes 884740
  0.7 11.6 %collective-permute-start.3 = (bf16[576,256]{1,0:T(8,128)(2,1)}, bf16[576,256]{1,0:T(8,128)(2,1)S(1)}, u32[]{:S(2)}, u32[]{:S(2)}) collective-permute-start(bf16[576,256]{1,0:T(8,128)(2,1)} %bitcast.1), channel_id=1, source_target_pairs={{16,0},{24,8},{0,16},{8,24},{48,32},{56,40},{32,48},{40,56},{80,64... | collective-permute-start | bytes 884744 | tf_op jit(solution)/shard_map/ppermute | solution.py:52
  3.2 9.1 %collective-permute-start.2 = (bf16[576,256]{1,0:T(8,128)(2,1)}, bf16[576,256]{1,0:T(8,128)(2,1)S(1)}, u32[]{:S(2)}, u32[]{:S(2)}) collective-permute-start(bf16[576,256]{1,0:T(8,128)(2,1)} %bitcast.2), channel_id=1, source_target_pairs={{8,0},{0,8},{24,16},{16,24},{40,32},{32,40},{56,48},{48,56},{72,64... | collective-permute-start | bytes 884744 | tf_op jit(solution)/shard_map/ppermute | solution.py:52
  4.2 15.6 %collective-permute-start.1 = (bf16[576,256]{1,0:T(8,128)(2,1)}, bf16[576,256]{1,0:T(8,128)(2,1)S(1)}, u32[]{:S(2)}, u32[]{:S(2)}) collective-permute-start(bf16[576,256]{1,0:T(8,128)(2,1)} %bitcast.3), channel_id=1, source_target_pairs={{248,0},{16,8},{8,16},{32,24},{24,32},{48,40},{40,48},{64,56},{56,... | collective-permute-start | bytes 884744 | tf_op jit(solution)/shard_map/ppermute | solution.py:52
  5.6 14.2 %collective-permute-start = (bf16[576,256]{1,0:T(8,128)(2,1)}, bf16[576,256]{1,0:T(8,128)(2,1)S(1)}, u32[]{:S(2)}, u32[]{:S(2)}) collective-permute-start(bf16[576,256]{1,0:T(8,128)(2,1)} %bitcast.4), channel_id=1, source_target_pairs={{240,0},{248,8},{32,16},{40,24},{16,32},{24,40},{64,48},{72,56},{4... | collective-permute-start | bytes 884744 | tf_op jit(solution)/shard_map/ppermute | solution.py:52
